TPU v7x, 32 devices: a whole 2x2x4 slice. The times are simulated.
32 devices in a mesh: gx: 8 (over z, y), gy: 4 (over x, core).
Axes of the slice: x: 2, y: 2, z: 4, core: 2. Of those that a mesh axis runs over, the one named last changes fastest.
Arguments:
- vorticity: float32 [8192, 8192], P('gx', 'gy'), may hold values from -6 to 6
- closure_kernel: float32 [3, 3, 3], replicated, may hold values from -1.5 to 1.5
Outputs:
- rate_field: float32 [8192, 8192], P('gx', 'gy')
All inputs are finite; a program needn't handle non-finite values.
Results may differ from a plain program's by a relative error of at most 0.0001.
Values sent between devices are 32-bit elements; how exact they have to be, the bound alone decides.
A program may use at most 256 MiB of HBM per device.

v0:
```python
import math

import jax
import jax.numpy as jnp
from jax import lax
from jax.sharding import PartitionSpec as P

GRID = 8192


VISCOSITY = 0.5
DRAG = 0.1
FORCE_AMP = 1.0
FORCE_WAVES = 4.0
EXACT = lax.Precision.HIGHEST


def padded(cells, sides, width):
    for axis, dim in sides:
        count = lax.axis_size(axis)
        head = lax.slice_in_dim(cells, 0, width, axis=dim)
        tail = lax.slice_in_dim(cells, cells.shape[dim] - width, cells.shape[dim], axis=dim)
        cells = jnp.concatenate(
            [
                lax.ppermute(tail, axis, [(i, (i + 1) % count) for i in range(count)]),
                cells,
                lax.ppermute(head, axis, [((i + 1) % count, i) for i in range(count)]),
            ],
            axis=dim,
        )
    return cells


def factors(length):
    leading = 1
    while leading * leading < length:
        leading = leading * 2
    return (leading, length // leading)


def phases(period, count_rows, count_cols, sign_value):
    indices = (
        jnp.arange(count_rows, dtype=jnp.int32)[:, None]
        * jnp.arange(count_cols, dtype=jnp.int32)[None, :]
        % period
    )
    angles = 2.0 * math.pi / period * indices.astype(jnp.float32)
    return (jnp.cos(angles), sign_value * jnp.sin(angles))


def block_table(table_real, table_imag):
    return jnp.stack([jnp.stack([table_real, table_imag]), jnp.stack([-table_imag, table_real])])


def twisted(pair, twist_real, twist_imag):
    return jnp.stack(
        [pair[0] * twist_real - pair[1] * twist_imag, pair[0] * twist_imag + pair[1] * twist_real]
    )


def forward_real(field):
    length = field.shape[-1]
    leading, trailing = factors(length)
    lead_shape = field.shape[:-1]
    folded = field.reshape((-1, leading, trailing))
    table_real, table_imag = phases(leading, leading, leading, -1.0)
    section = jnp.einsum(
        "lab,pac->plcb", folded, jnp.stack([table_real, table_imag]), precision=EXACT
    )
    twist_real, twist_imag = phases(length, leading, trailing, -1.0)
    section = twisted(section, twist_real, twist_imag)
    final_real, final_imag = phases(trailing, trailing, trailing // 2, -1.0)
    spectrum = jnp.einsum(
        "plcb,pqbd->qldc", section, block_table(final_real, final_imag), precision=EXACT
    )
    half_length = trailing // 2 * leading
    return spectrum.reshape((2,) + lead_shape + (half_length,))


def complex_transform(pair, sign_value):
    length = pair.shape[-1]
    leading, trailing = factors(length)
    full_shape = pair.shape
    folded = pair.reshape((2, -1, leading, trailing))
    table_real, table_imag = phases(leading, leading, leading, sign_value)
    section = jnp.einsum(
        "plab,pqac->qlcb", folded, block_table(table_real, table_imag), precision=EXACT
    )
    twist_real, twist_imag = phases(length, leading, trailing, sign_value)
    section = twisted(section, twist_real, twist_imag)
    final_real, final_imag = phases(trailing, trailing, trailing, sign_value)
    result = jnp.einsum(
        "plcb,pqbd->qldc", section, block_table(final_real, final_imag), precision=EXACT
    )
    return result.reshape(full_shape)


def inverse_real(pair, length):
    leading, trailing = factors(length)
    lead_shape = pair.shape[1:-1]
    rows_half = leading // 2
    weights = (
        jnp.where(jnp.arange(rows_half * trailing) == 0, 1.0, 2.0)
        .astype(jnp.float32)
        .reshape(rows_half, trailing)
    )
    folded = pair.reshape((2, -1, rows_half, trailing)) * weights
    table_real, table_imag = phases(leading, rows_half, leading, 1.0)
    section = jnp.einsum(
        "plab,pqac->qlcb", folded, block_table(table_real, table_imag), precision=EXACT
    )
    twist_real, twist_imag = phases(length, leading, trailing, 1.0)
    section = twisted(section, twist_real, twist_imag)
    final_real, final_imag = phases(trailing, trailing, trailing, 1.0)
    field = jnp.einsum(
        "plcb,pbd->ldc", section, jnp.stack([final_real, -final_imag]), precision=EXACT
    )
    return field.reshape(lead_shape + (length,)) * (1.0 / length)


def velocity(line_field):
    packed = forward_real(line_field)
    blocked = lax.all_to_all(packed, "gy", split_axis=2, concat_axis=1, tiled=True)
    blocked = jnp.swapaxes(blocked, 1, 2)
    columns = lax.all_to_all(blocked, "gx", split_axis=1, concat_axis=2, tiled=True)
    wave = complex_transform(columns, -1.0)
    wave_count = columns.shape[1]
    grid_length = columns.shape[2]
    band_width = blocked.shape[1]
    index_second = (
        lax.axis_index("gy") * band_width
        + lax.axis_index("gx") * wave_count
        + jnp.arange(wave_count, dtype=jnp.int32)
    )
    index_first = jnp.arange(grid_length, dtype=jnp.int32)
    index_first = jnp.where(index_first < grid_length // 2, index_first, index_first - grid_length)
    number_second = (2.0 * math.pi / grid_length * index_second.astype(jnp.float32))[:, None]
    number_first = (2.0 * math.pi / grid_length * index_first.astype(jnp.float32))[None, :]
    squared = number_first**2 + number_second**2
    positive = squared > 0.0
    inverse = jnp.where(positive, 1.0 / jnp.where(positive, squared, 1.0), 0.0)
    potential = wave * inverse
    spectral = jnp.stack(
        [
            jnp.stack([-number_second * potential[1], number_first * potential[1]]),
            jnp.stack([number_second * potential[0], -number_first * potential[0]]),
        ]
    )
    back = complex_transform(spectral, 1.0) * (1.0 / grid_length)
    returned = lax.all_to_all(back, "gx", split_axis=3, concat_axis=2, tiled=True)
    returned = jnp.swapaxes(returned, 2, 3)
    lines_back = lax.all_to_all(returned, "gy", split_axis=2, concat_axis=3, tiled=True)
    return inverse_real(lines_back, grid_length)


def tendency(extended, closure_kernel, column_start):
    vortex = extended[0]
    centre = vortex[1:-1, 1:-1]
    rows_count = centre.shape[0]
    cols_count = centre.shape[1]
    x_minus = vortex[:-2, 1:-1]
    x_plus = vortex[2:, 1:-1]
    y_minus = vortex[1:-1, :-2]
    y_plus = vortex[1:-1, 2:]
    speed_first = extended[1, 1:-1, 1:-1]
    speed_second = extended[2, 1:-1, 1:-1]
    advect = jnp.maximum(speed_first, 0.0) * (centre - x_minus) + jnp.minimum(speed_first, 0.0) * (
        x_plus - centre
    )
    advect = (
        advect
        + jnp.maximum(speed_second, 0.0) * (centre - y_minus)
        + jnp.minimum(speed_second, 0.0) * (y_plus - centre)
    )
    laplace = x_plus + x_minus + y_plus + y_minus - 4.0 * centre
    closure = jnp.zeros_like(centre)
    for channel in range(3):
        for shift_row in range(3):
            for shift_col in range(3):
                closure = (
                    closure
                    + closure_kernel[channel, shift_row, shift_col]
                    * extended[
                        channel,
                        shift_row : shift_row + rows_count,
                        shift_col : shift_col + cols_count,
                    ]
                )
    columns = (column_start + jnp.arange(cols_count, dtype=jnp.int32)).astype(jnp.float32)
    forcing = FORCE_AMP * jnp.cos(2.0 * math.pi * FORCE_WAVES / GRID * columns)
    return -advect + VISCOSITY * laplace - DRAG * centre + forcing[None, :] + closure


def per_device(vorticity, closure_kernel):
    line_field = lax.all_to_all(vorticity, "gy", split_axis=0, concat_axis=1, tiled=True)
    speeds = velocity(line_field)
    speeds = lax.all_to_all(speeds, "gy", split_axis=2, concat_axis=1, tiled=True)
    stacked = jnp.concatenate([vorticity[None], speeds], axis=0)
    extended = padded(stacked, (("gx", 1), ("gy", 2)), 1)
    return tendency(extended, closure_kernel, lax.axis_index("gy") * vorticity.shape[1])


def solution(mesh):
    placed = (P("gx", "gy"), P())
    return jax.shard_map(
        per_device, mesh=mesh, in_specs=placed, out_specs=P("gx", "gy"), check_vma=False
    )
```

profile of v0, /device:TPU:0, one launch (start us, length us, event | category | flops | bytes accessed | tf_op | source)
XLA Modules:
  0.0 2182.0 jit_solution(12848783397649653239)
XLA Ops:
  6.3 93.2 %all-to-all-done = f32[4,256,2048]{2,1,0:T(8,128)} async-done(((f32[4,256,2048]{2,1,0:T(8,128)}), f32[4,256,2048]{2,1,0:T(8,128)}, u32[]{:S(2)}, u32[]{:S(2)}) %all-to-all-start) | async-done | bytes 8388640 | tf_op jit(solution)/shard_map/all_to_all | solution.py:195
  189.5 97.2 %all_to_all.100 = f32[2,256,4096]{1,0,2:T(2,128)S(1)} all-to-all(f32[2,256,4096]{1,0,2:T(2,128)} %bitcast.416), channel_id=1, replica_groups=mesh['gx'=8,'gy'=4] {'gy'}, dimensions={2} | all-to-all | bytes 16777216 | tf_op jit(solution)/shard_map/all_to_all | solution.py:123
  325.5 176.7 %all-to-all-done.2 = f32[2,1024,1024]{2,0,1:T(2,128)} async-done(((f32[2,1024,1024]{2,0,1:T(2,128)}), f32[2,1024,1024]{2,0,1:T(2,128)}, u32[]{:S(2)}, u32[]{:S(2)}) %all-to-all-start.2) | async-done | bytes 8388640 | tf_op jit(solution)/shard_map/all_to_all | solution.py:125
  585.4 31.2 %slice_multiply_fusion.5 = (f32[1,128,8192]{1,0,2:T(1,128)S(1)}, f32[1,128,8192]{1,0,2:T(1,128)S(1)}, f32[1,128,8192]{1,0,2:T(1,128)}, f32[1,128,8192]{1,0,2:T(1,128)}) fusion(f32[2,128,8192]{1,0,2:T(2,128)S(1)} %bitcast_multiply_fusion.6, f32[128]{0:T(128)S(1)} %fusion.204, f32[8192]{0:T(1024)S(1)} %get-tuple-element.80, f32[8192]{0:T(1024)S(1)} %get-tuple-element.81, ...), kind=kLoop, calls=%fused_computation.198 | loop fusion | flops 4194304 | bytes 25232384 | tf_op jit(solution)/shard_map/mul | solution.py:145
  677.0 23.0 %fusion.110 = f32[2,256,128,64]{1,2,3,0:T(8,128)} fusion(f32[1,256,128,64]{2,1,0,3:T(8,128)} %copy.227, f32[1,256,128,64]{2,1,0,3:T(8,128)} %copy.226, f32[1,2,128,128]{2,3,1,0:T(8,128)S(1)} %get-tuple-element.30, f32[1,2,128,128]{2,3,1,0:T(8,128)S(1)} %get-tuple-element.27), kind=kOutput, calls=%fused_computation.185 | convolution fusion | flops 12889161728 | bytes 33816576 | tf_op jit(solution)/shard_map/plab,pqac->qlcb/dot_general | solution.py:86
  730.5 22.7 %fusion.5 = f32[2,256,64,128]{3,2,1,0:T(8,128)} fusion(f32[2,256,128,64]{2,3,0,1:T(8,128)} %copy.230, f32[1,2,64,64]{2,3,1,0:T(8,128)S(1)} %get-tuple-element.36, f32[1,2,64,64]{2,3,1,0:T(8,128)S(1)} %get-tuple-element.33), kind=kOutput, calls=%fused_computation.49 | convolution fusion | flops 6446661632 | bytes 33619968 | tf_op jit(solution)/shard_map/plcb,pqbd->qldc/dot_general | solution.py:92
  753.2 18.2 mul.1280
  771.4 25.0 %copy.231 = f32[2,2,128,8192]{2,1,0,3:T(2,128)} copy(f32[2,2,128,8192]{3,2,1,0:T(8,128)} %mul.1280) | data formatting | bytes 33554432 | tf_op jit(solution)/shard_map/mul | solution.py:149
  796.4 367.4 %all_to_all.101 = f32[2,2,128,8192]{2,1,0,3:T(2,128)S(1)} all-to-all(f32[2,2,128,8192]{2,1,0,3:T(2,128)} %copy.231), channel_id=1, replica_groups=mesh['gx'=8,'gy'=4] {'gx'}, dimensions={3} | all-to-all | bytes 33554432 | tf_op jit(solution)/shard_map/all_to_all | solution.py:150
  1186.5 25.4 %copy.234 = f32[2,2,1024,1024]{3,1,0,2:T(2,128)} copy(f32[2,2,1024,1024]{2,3,1,0:T(8,128)} %bitcast.413) | data formatting | bytes 33554432 | tf_op jit(solution)/shard_map/transpose | solution.py:151
  1219.5 182.7 %all-to-all-done.4 = f32[2,2,1024,1024]{3,1,0,2:T(2,128)} async-done(((f32[2,2,1024,1024]{3,1,0,2:T(2,128)}), f32[2,2,1024,1024]{3,1,0,2:T(2,128)}, u32[]{:S(2)}, u32[]{:S(2)}) %all-to-all-start.4) | async-done | bytes 16777248 | tf_op jit(solution)/shard_map/all_to_all | solution.py:152
  1402.2 32.9 %copy.235 = f32[2,2,4,256,1024]{3,1,4,2,0:T(2,128)} copy(f32[2,2,4,256,1024]{4,1,0,3,2:T(2,128)} %bitcast.67) | data formatting | bytes 33554432 | tf_op jit(solution)/shard_map/all_to_all | solution.py:152
  1435.0 21.6 reshape.609
  1463.3 37.2 %convolution_bitcast_fusion = f32[2,512,128,64]{1,2,3,0:T(8,128)} fusion(f32[2,512,64,64]{1,3,2,0:T(8,128)S(1)} %broadcast_multiply_fusion, f32[1,2,64,128]{3,2,0,1:T(8,128)S(1)} %get-tuple-element.32, f32[1,2,64,128]{3,2,0,1:T(8,128)S(1)} %get-tuple-element.31), kind=kOutput, calls=%fused_computation.38 | convolution fusion | flops 12884934656 | bytes 50462720 | tf_op jit(solution)/shard_map/plab,pqac->qlcb/dot_general | solution.py:109
  1518.1 18.8 pad_maximum_fusion.1
  1536.9 32.5 %copy.237 = f32[2,512,128,64]{2,3,0,1:T(8,128)} copy(f32[2,512,128,64]{1,2,3,0:T(8,128)} %pad_maximum_fusion.1) | data formatting | bytes 67108864 | tf_op jit(solution)/shard_map/stack | solution.py:56
  1569.4 24.6 %fusion.3 = f32[512,64,128]{2,1,0:T(8,128)} fusion(f32[2,512,128,64]{2,3,0,1:T(8,128)} %copy.237, f32[1,64,64]{1,2,0:T(8,128)S(1)} %copy-done.2, f32[1,64,64]{1,2,0:T(8,128)S(1)} %copy-done.4), kind=kOutput, calls=%fused_computation.46 | convolution fusion | flops 6446653440 | bytes 50364416 | tf_op jit(solution)/shard_map/plcb,pbd->ldc/dot_general | solution.py:115
  1612.2 25.0 %copy.238 = f32[2,256,8192]{1,0,2:T(2,128)} copy(f32[2,256,8192]{2,1,0:T(8,128)} %mul.1292) | data formatting | bytes 33554432 | tf_op jit(solution)/shard_map/mul | solution.py:118
  1645.9 181.6 %all-to-all-done.5 = f32[2,256,8192]{1,0,2:T(2,128)} async-done(((f32[2,256,8192]{1,0,2:T(2,128)}), f32[2,256,8192]{1,0,2:T(2,128)}, u32[]{:S(2)}, u32[]{:S(2)}) %all-to-all-start.5) | async-done | bytes 16777248 | tf_op jit(solution)/shard_map/all_to_all | solution.py:197
  1827.5 25.1 %copy.240 = f32[2,256,4,2048]{3,1,2,0:T(8,128)} copy(f32[2,256,4,2048]{1,0,3,2:T(2,128)} %bitcast.77) | data formatting | bytes 33554432 | tf_op jit(solution)/shard_map/all_to_all | solution.py:197
  1870.8 65.8 %concatenate.43 = f32[3,1026,2048]{2,1,0:T(8,128)} concatenate(f32[3,1,2048]{2,1,0:T(1,128)S(1)} %collective-permute-done, f32[3,1024,2048]{2,1,0:T(8,128)} %pad_maximum_fusion, f32[3,1,2048]{2,1,0:T(1,128)S(1)} %collective-permute-done.1), dimensions={1} | concatenate | bytes 50429952 | tf_op jit(solution)/shard_map/concatenate | solution.py:23
  1940.6 24.3 %slice_maximum_fusion.1 = (f32[1,4,256,2048]{3,2,1,0:T(8,128)}, f32[1,4,256,2048]{3,2,1,0:T(8,128)}, f32[1,4,256,2048]{3,2,1,0:T(8,128)}, f32[1,4,256,2048]{3,2,...) fusion(f32[2,4,256,2048]{3,2,1,0:T(8,128)} %bitcast.405, f32[]{:T(128)} %bitcast.108, f32[]{:T(128)} %bitcast.126), kind=kLoop, calls=%fused_computation.183 | loop fusion | flops 12582912 | bytes 67108872 | tf_op jit(solution)/shard_map/max | solution.py:167
  1965.9 31.7 %concatenate.44 = f32[3,1026,2050]{2,1,0:T(8,128)} concatenate(f32[3,1026,1]{2,1,0:T(8,128)S(1)} %copy.243, f32[3,1026,2048]{2,1,0:T(8,128)} %concatenate.43, f32[3,1026,1]{2,1,0:T(8,128)S(1)} %copy.244), dimensions={2} | concatenate | bytes 50479200 | tf_op jit(solution)/shard_map/concatenate | solution.py:23
  2005.2 176.3 %fusion.18 = f32[1024,2048]{1,0:T(8,128)} fusion(f32[3,1026,2048]{2,1,0:T(8,128)} %concatenate.43, f32[3,1026,1]{2,1,0:T(8,128)S(1)} %copy.244, f32[3,1,2048]{2,1,0:T(1,128)S(1)} %collective-permute-done.1, f32[2,1024,2048]{2,1,0:T(8,128)} %bitcast.406, f32[1,1024,2048]{2,1,0:T(8,128)} %bitcast.411, f32[3,1026,1]{2,1,0:T(8,128)S(1)} %copy.243, ...), kind=kLoop, calls=%fused_computation.65 | loop fusion | flops 218103808 | bytes 159514768 | tf_op jit(solution)/shard_map/add | solution.py:191
  (92 shorter events, 421.2 us)
Async XLA Ops:
  0.0 99.5 %all-to-all-start = ((f32[4,256,2048]{2,1,0:T(8,128)}), f32[4,256,2048]{2,1,0:T(8,128)}, u32[]{:S(2)}, u32[]{:S(2)}) async-start(f32[4,256,2048]{2,1,0:T(8,128)} %bitcast.408), calls=%async_computation | async-start | bytes 16777216 | tf_op jit(solution)/shard_map/all_to_all | solution.py:195
  312.8 189.4 %all-to-all-start.2 = ((f32[2,1024,1024]{2,0,1:T(2,128)}), f32[2,1024,1024]{2,0,1:T(2,128)}, u32[]{:S(2)}, u32[]{:S(2)}) async-start(f32[2,1024,1024]{2,0,1:T(2,128)} %copy.219), calls=%async_computation.2 | async-start | bytes 16777216 | tf_op jit(solution)/shard_map/all_to_all | solution.py:125
  320.2 0.6 copy-start.1
  320.2 0.6 copy-start.3
  1211.9 190.2 %all-to-all-start.4 = ((f32[2,2,1024,1024]{3,1,0,2:T(2,128)}), f32[2,2,1024,1024]{3,1,0,2:T(2,128)}, u32[]{:S(2)}, u32[]{:S(2)}) async-start(f32[2,2,1024,1024]{3,1,0,2:T(2,128)} %copy.234), calls=%async_computation.4 | async-start | bytes 33554432 | tf_op jit(solution)/shard_map/all_to_all | solution.py:152
  1536.9 32.5 %copy-start.2 = (f32[1,64,64]{1,2,0:T(8,128)S(1)}, f32[1,64,64]{1,2,0:T(8,128)}, u32[]{:S(2)}) copy-start(f32[1,64,64]{1,2,0:T(8,128)} %copy-done.1) | copy-start | bytes 49156
  1536.9 32.5 %copy-start.4 = (f32[1,64,64]{1,2,0:T(8,128)S(1)}, f32[1,64,64]{1,2,0:T(8,128)}, u32[]{:S(2)}) copy-start(f32[1,64,64]{1,2,0:T(8,128)} %copy-done.3) | copy-start | bytes 49156
  1637.3 7.2 copy-start.5
  1637.3 190.2 %all-to-all-start.5 = ((f32[2,256,8192]{1,0,2:T(2,128)}), f32[2,256,8192]{1,0,2:T(2,128)}, u32[]{:S(2)}, u32[]{:S(2)}) async-start(f32[2,256,8192]{1,0,2:T(2,128)} %copy.238), calls=%async_computation.5 | async-start | bytes 33554432 | tf_op jit(solution)/shard_map/all_to_all | solution.py:197
  1852.5 6.0 copy-start
  1853.7 17.1 collective-permute-start.1
  1855.3 15.6 collective-permute-start
  1940.0 25.3 %collective-permute-start.3 = (f32[3,1026,1]{1,2,0:T(1,128)S(1)}, f32[3,1026,1]{1,2,0:T(1,128)S(1)}, u32[]{:S(2)}, u32[]{:S(2)}) collective-permute-start(f32[3,1026,1]{1,2,0:T(1,128)S(1)} %copy.242), channel_id=1, source_target_pairs={{1,0},{2,1},{3,2},{0,3},{5,4},{6,5},{7,6},{4,7},{9,8},{10,9},{11,1... | collective-permute-start | bytes 36944 | tf_op jit(solution)/shard_map/ppermute | solution.py:27
  1940.1 24.8 %collective-permute-start.2 = (f32[3,1026,1]{1,2,0:T(1,128)S(1)}, f32[3,1026,1]{1,2,0:T(1,128)S(1)}, u32[]{:S(2)}, u32[]{:S(2)}) collective-permute-start(f32[3,1026,1]{1,2,0:T(1,128)S(1)} %copy.241), channel_id=1, source_target_pairs={{0,1},{1,2},{2,3},{3,0},{4,5},{5,6},{6,7},{7,4},{8,9},{9,10},{10,1... | collective-permute-start | bytes 36944 | tf_op jit(solution)/shard_map/ppermute | solution.py:25
where the time goes:
time: 2200 us; the launch traced here: 2180 us
  waiting for transfers between devices  634 us (29%)
  local copies, waits for them, and re-layouts  535 us (24%)
  blocking collectives  465 us (21%)
  other arithmetic  358 us (16%)
  matrix products  160 us (7%)
  starting transfers between devices  29.2 us (1%)
    all_to_all x1, blocking collectives, velocity(): lax.all_to_all(back, 'gx', split_axis=3, concat_axis=2, tiled=True)  367 us
    all_to_all x1, waiting for transfers between devices, velocity(): lax.all_to_all(returned, 'gy', split_axis=2, concat_axis=3, tiled=True)  183 us
    all_to_all x1, waiting for transfers between devices, per_device(): lax.all_to_all(speeds, 'gy', split_axis=2, concat_axis=1, tiled=True)  182 us
    all_to_all x1, waiting for transfers between devices, velocity(): lax.all_to_all(blocked, 'gx', split_axis=1, concat_axis=2, tiled=True)  177 us
    add x1, other arithmetic, tendency(): -advect + VISCOSITY * laplace - DRAG * centre + forcing[None, :] + closure  176 us
    concatenate x2, local copies, waits for them, and re-layouts, padded(): jnp.concatenate([lax.ppermute(tail, axis, [(i, (i + 1) % count) for i in...  97.5 us
    all_to_all x1, blocking collectives, velocity(): lax.all_to_all(packed, 'gy', split_axis=2, concat_axis=1, tiled=True)  97.2 us
    all_to_all x1, waiting for transfers between devices, per_device(): lax.all_to_all(vorticity, 'gy', split_axis=0, concat_axis=1, tiled=True)  93.2 us
  transfers between devices with their start and end apart: 8, of which 4 were waited for; matrix products, arithmetic and copies ran while one was open for 2% of the time, Pallas kernels for 0%

commit v1 on v0

v1 whole, which is shorter than its diff:
```python
import functools
import math

import jax
import jax.numpy as jnp
import numpy as np
from jax import lax
from jax.experimental import pallas as pl
from jax.experimental.pallas import tpu as pltpu
from jax.sharding import PartitionSpec as P

VISCOSITY = 0.5
DRAG = 0.1
FORCE_AMP = 1.0
FORCE_WAVES = 4.0
TAIL = 64
NEAR = lax.Precision.HIGH
BOTH = ("gx", "gy")


def turns(period, *indices):
    product = functools.reduce(lambda a, b: a * b, np.ix_(*indices)) % period
    return np.exp(2j * np.pi / period * product)


def real_form(table, out_axis, in_axis):
    rows = [
        np.stack([table.real, -table.imag], axis=in_axis),
        np.stack([table.imag, table.real], axis=in_axis),
    ]
    return np.stack(rows, axis=out_axis).astype(np.float32)


def head_forward(lead):
    return real_form(turns(lead, np.arange(lead), np.arange(lead)).conj(), 1, 1)


def tail_forward(length, lead, kept):
    tail = length // lead
    c, b, d = np.arange(lead), np.arange(tail), np.arange(kept)
    table = turns(tail, d, b)[None] * turns(length, c, b)[:, None, :]
    real = real_form(table.conj(), 1, 2)
    return real.reshape(lead, 2 * kept, 2 * tail)


def tail_inverse(length, lead, weights):
    tail = length // lead
    c, b, d = np.arange(lead), np.arange(tail), np.arange(weights.shape[1])
    table = turns(tail, b, d)[None] * turns(length, c, b)[:, :, None] * weights[:, None, :]
    real = real_form(table, 1, 2)
    return real.reshape(lead, 2 * tail, 2 * weights.shape[1])


def head_product(table, cells):
    return jnp.einsum("rh,hbk->rbk", table, cells, precision=NEAR)


def tail_product(table, cells):
    return jnp.einsum("cmn,cnk->cmk", table, cells, precision=NEAR)


def stencil_kernel(grid_length, weights, *refs):
    out_ref = refs[-1]
    rows = out_ref.shape[0]
    fields = [refs[3 * i : 3 * i + 3] for i in range(3)]
    halo = jnp.concatenate([ref[...] for ref in refs[9:12]], axis=0)
    turned = [None, None, None]
    shifted = []
    for channel in range(3):
        mid, before, after = fields[channel]
        centre = jnp.concatenate([before[...], mid[...], after[...]], axis=0)
        minus = jnp.concatenate([halo[:, 2 * channel : 2 * channel + 1], centre[:, :-1]], axis=1)
        plus = jnp.concatenate([centre[:, 1:], halo[:, 2 * channel + 1 : 2 * channel + 2]], axis=1)
        trio = (minus, centre, plus)
        shifted.append(trio)
        for shift_second in range(3):
            for shift_first in range(3):
                term = weights[channel * 9 + shift_first * 3 + shift_second] * trio[shift_first]
                known = turned[shift_second]
                turned[shift_second] = term if known is None else known + term
    closure = turned[0][7 : 7 + rows] + turned[1][8 : 8 + rows] + turned[2][9 : 9 + rows]
    x_minus, whole, x_plus = shifted[0]
    x_minus, x_plus = x_minus[8 : 8 + rows], x_plus[8 : 8 + rows]
    centre = whole[8 : 8 + rows]
    y_minus, y_plus = whole[7 : 7 + rows], whole[9 : 9 + rows]
    first, second = fields[1][0][...], fields[2][0][...]
    advect = jnp.maximum(first, 0.0) * (centre - x_minus) + jnp.minimum(first, 0.0) * (x_plus - centre)
    advect += jnp.maximum(second, 0.0) * (centre - y_minus) + jnp.minimum(second, 0.0) * (y_plus - centre)
    laplace = x_plus + x_minus + y_plus + y_minus - 4.0 * centre
    force = refs[12][...]
    out_ref[...] = closure - advect + VISCOSITY * laplace - DRAG * centre + force


def stencil(field, first, second, halo, force, closure_kernel):
    length, width = field.shape
    rows = 128
    steps = rows // 8
    last = length // 8

    def specs(columns):
        return [
            pl.BlockSpec((rows, columns), lambda i: (i, 0)),
            pl.BlockSpec((8, columns), lambda i: ((i * steps + last - 1) % last, 0)),
            pl.BlockSpec((8, columns), lambda i: ((i * steps + steps) % last, 0)),
        ]

    halo_specs = specs(halo.shape[1])

    def body(weights_ref, *refs):
        weights = [weights_ref[i] for i in range(27)]
        stencil_kernel(length, weights, *refs)

    return pl.pallas_call(
        body,
        grid=(length // rows,),
        in_specs=[pl.BlockSpec(memory_space=pltpu.SMEM)]
        + specs(width) * 3
        + [halo_specs[1], halo_specs[0], halo_specs[2]]
        + [pl.BlockSpec((rows, 1), lambda i: (i, 0))],
        out_specs=pl.BlockSpec((rows, width), lambda i: (i, 0)),
        out_shape=jax.ShapeDtypeStruct((length, width), jnp.float32),
        compiler_params=pltpu.CompilerParams(vmem_limit_bytes=32 * 1024 * 1024),
    )(closure_kernel.reshape(27), *([field] * 3), *([first] * 3), *([second] * 3), *([halo] * 3), force)


def edges(cells):
    count = lax.axis_size("gx") * lax.axis_size("gy")
    onward = [(i, (i + 1) % count) for i in range(count)]
    backward = [((i + 1) % count, i) for i in range(count)]
    from_left = lax.ppermute(cells[..., -1], BOTH, onward)
    from_right = lax.ppermute(cells[..., 0], BOTH, backward)
    return from_left, from_right


def per_device(vorticity, closure_kernel):
    parts = lax.axis_size("gy")
    devices = lax.axis_size("gx") * parts
    rows, columns = vorticity.shape
    length = columns * parts
    width = rows // parts
    tail = min(TAIL, width)
    lead = length // tail
    half = tail // 2
    bands = lead // devices
    waves = bands * half
    folds = width // tail

    turned = vorticity.reshape(parts, width, columns).swapaxes(1, 2)
    field = lax.all_to_all(turned, "gy", 0, 0).reshape(length, width)

    head = head_forward(lead)
    section = head_product(
        head[:, :, 0, :].reshape(2 * lead, lead), field.reshape(lead, tail, width)
    )
    section = tail_product(
        tail_forward(length, lead, half), section.reshape(lead, 2 * tail, width)
    )
    section = section.reshape(devices, bands, 2, half, width).transpose(0, 2, 4, 1, 3)
    lines = lax.all_to_all(section.reshape(devices, 2, width, waves), BOTH, 0, 0)

    mixed = head.reshape(lead, 2, 2, devices, folds).transpose(0, 1, 3, 2, 4)
    wave = head_product(
        mixed.reshape(2 * lead, 2 * lead), lines.reshape(2 * lead, tail, waves)
    )
    wave = tail_product(
        tail_forward(length, lead, tail), wave.reshape(lead, 2 * tail, waves)
    ).reshape(lead, 2, tail, waves)

    unit = 2.0 * math.pi / length
    mode = np.arange(lead)[:, None] + lead * np.arange(tail)[None, :]
    mode = np.where(mode < length // 2, mode, mode - length)
    number_first = jnp.asarray(unit * mode, jnp.float32)[:, :, None]
    local = lax.axis_index(BOTH) * bands + jnp.arange(waves, dtype=jnp.int32) // half
    number_second = unit * (local + lead * (jnp.arange(waves, dtype=jnp.int32) % half)).astype(jnp.float32)
    squared = number_first**2 + number_second**2
    positive = squared > 0.0
    inverse = jnp.where(positive, 1.0 / jnp.where(positive, squared, 1.0), 0.0)
    potential = wave * inverse[:, None]
    spectral = jnp.concatenate(
        [potential * number_second, potential * -number_first[:, None]], axis=-1
    )

    even = np.full((lead, tail), 1.0 / length)
    back = tail_product(
        tail_inverse(length, lead, even), spectral.reshape(lead, 2 * tail, 2 * waves)
    )
    head_back = head.reshape(lead, 2, 2, lead).transpose(3, 2, 0, 1)
    mixed_back = head_back.reshape(devices, folds, 2, lead, 2).transpose(0, 2, 1, 3, 4)
    back = head_product(
        mixed_back.reshape(2 * lead, 2 * lead), back.reshape(2 * lead, tail, 2 * waves)
    )
    lines = lax.all_to_all(back.reshape(devices, 2, width, 2 * waves), BOTH, 0, 0)

    lines = lines.reshape(devices, 2, width, 2, bands, half).transpose(0, 4, 1, 5, 3, 2)
    uneven = np.full((lead, half), 2.0 / length)
    uneven[0, 0] = 1.0 / length
    speeds = tail_product(
        tail_inverse(length, lead, uneven), lines.reshape(lead, 2 * half, 2 * width)
    )
    last = -head_back[:, 1].reshape(lead, 2 * lead)
    speeds = head_product(last, speeds.reshape(2 * lead, tail, 2 * width))
    first = speeds[..., :width].reshape(length, width)
    second = speeds[..., width:].reshape(length, width)

    halo = []
    for cells in (field, first, second):
        halo.extend(edges(cells))
    halo = jnp.stack(halo, axis=-1)
    force = FORCE_AMP * np.cos(2.0 * np.pi * FORCE_WAVES / length * np.arange(length))
    force = jnp.asarray(force, jnp.float32)[:, None]
    rate = stencil(field, first, second, halo, force, closure_kernel)

    rate = lax.all_to_all(rate.reshape(parts, columns, width), "gy", 0, 0)
    return rate.swapaxes(1, 2).reshape(rows, columns)


def solution(mesh):
    placed = (P("gx", "gy"), P())
    return jax.shard_map(
        per_device, mesh=mesh, in_specs=placed, out_specs=P("gx", "gy"), check_vma=False
    )
```

time: 2200 us -> 1220 us (0.55)
  other arithmetic: 358 us -> 1.16 us
  local copies, waits for them, and re-layouts: 535 us -> 206 us
  blocking collectives: 465 us -> 198 us
  waiting for transfers between devices: 634 us -> 533 us
  Pallas kernels: 0 us -> 55.8 us
  matrix products: 160 us -> 187 us
    all_to_all x2, blocking collectives: 465 us -> 198 us  [the longest x1 101 us: per_device(): field = lax.all_to_all(turned, 'gy', 0, 0).reshape(length, width)]
    add x1 -> x0, other arithmetic: 176 us -> none  [tendency(): -advect + VISCOSITY * laplace - DRAG * centre + forcing[None, :] + closure]
    another operation x8 -> x2, local copies, waits for them, and re-layouts: 116 us -> 2.94 us  [per_device(): halo = jnp.stack(halo, axis=-1)]
    all_to_all x4 -> x2, waiting for transfers between devices: 634 us -> 532 us  [the longest x1 361 us: per_device(): lax.all_to_all(back.reshape(devices, 2, width, 2 * waves), BOTH, 0, 0)]
    concatenate x2 -> x0, local copies, waits for them, and re-layouts: 97.5 us -> none  [padded(): jnp.concatenate([lax.ppermute(tail, axis, [(i, (i + 1) % count) for i in...]
    all_to_all x9 -> x3, local copies, waits for them, and re-layouts: 120 us -> 35.1 us  [the longest x1 17.4 us: per_device(): lax.all_to_all(back.reshape(devices, 2, width, 2 * waves), BOTH, 0, 0)]
    mul x4, local copies, waits for them, and re-layouts: 86.4 us -> 13.7 us  [the longest x2 13.6 us: per_device(): potential = wave * inverse[:, None]]
    another operation x10 -> x0, other arithmetic: 57.7 us -> none  [the longest x4 39 us: twisted(): jnp.stack([pair[0] * twist_real - pair[1] * twist_imag, pair[0] * twist_i...]
  transfers between devices with their start and end apart: 8 -> 8, of which waited for: 4 -> 3; matrix products, arithmetic and copies ran while one was open for 2% -> 15% of each run, Pallas kernels for 0% -> 0%
where the time goes in v1:
time: 1220 us; the launch traced here: 1210 us
  waiting for transfers between devices  533 us (44%)
  local copies, waits for them, and re-layouts  206 us (17%)
  blocking collectives  198 us (16%)
  matrix products  187 us (15%)
  Pallas kernels  55.8 us (5%)
  starting transfers between devices  26.1 us (2%)
    all_to_all x1, waiting for transfers between devices, per_device(): lax.all_to_all(back.reshape(devices, 2, width, 2 * waves), BOTH, 0, 0)  361 us
    all_to_all x1, waiting for transfers between devices, per_device(): lax.all_to_all(section.reshape(devices, 2, width, waves), BOTH, 0, 0)  171 us
    dot_general x4, matrix products, head_product(): return jnp.einsum('rh,hbk->rbk', table, cells, precision=NEAR)  112 us
    all_to_all x1, blocking collectives, per_device(): field = lax.all_to_all(turned, 'gy', 0, 0).reshape(length, width)  101 us
    all_to_all x1, blocking collectives, per_device(): rate = lax.all_to_all(rate.reshape(parts, columns, width), 'gy', 0, 0)  96.9 us
    dot_general x4, matrix products, tail_product(): return jnp.einsum('cmn,cnk->cmk', table, cells, precision=NEAR)  74.9 us
    pallas_call x1, Pallas kernels, stencil(): pl.pallas_call(body, grid=(length // rows,), in_specs=[pl.BlockSpec(memor...  55.8 us
    dot_general x3, local copies, waits for them, and re-layouts, head_product(): return jnp.einsum('rh,hbk->rbk', table, cells, precision=NEAR)  46 us
  transfers between devices with their start and end apart: 8, of which 3 were waited for; matrix products, arithmetic and copies ran while one was open for 15% of the time, Pallas kernels for 0%

profile of v1, /device:TPU:0, one launch (start us, length us, event | category | flops | bytes accessed | tf_op | source)
XLA Modules:
  0.0 1208.5 jit_solution(14352158528797423589)
XLA Ops:
  0.0 101.2 %all_to_all.20 = f32[4,2048,256]{1,2,0:T(8,128)} all-to-all(f32[4,2048,256]{1,2,0:T(8,128)} %bitcast.71), channel_id=1, replica_groups=mesh['gx'=8,'gy'=4] {'gy'}, dimensions={0} | all-to-all | bytes 16777216 | tf_op jit(solution)/shard_map/all_to_all | solution.py:149
  101.2 8.7 copy.70
  109.9 14.9 %fusion.10 = f32[256,64,256]{2,0,1:T(8,128)S(1)} fusion(f32[256,128,1]{1,0,2:T(8,128)S(1)} %copy-done.7, f32[128,64,256]{2,1,0:T(8,128)} %bitcast.47), kind=kOutput, calls=%fused_computation.10 | convolution fusion | flops 3221225472 | bytes 25296896 | tf_op jit(solution)/shard_map/rh,hbk->rbk/dot_general | solution.py:55
  124.8 20.3 %copy.73 = f32[256,64,256]{2,1,0:T(8,128)} copy(f32[256,64,256]{2,0,1:T(8,128)S(1)} %fusion.10) | data formatting | bytes 33554432 | tf_op jit(solution)/shard_map/rh,hbk->rbk/dot_general | solution.py:55
  145.1 15.9 %fusion.22 = f32[128,64,256]{2,1,0:T(8,128)} fusion(f32[128,64,128]{2,1,0:T(8,128)} %constant.78.clone, f32[128,128,256]{2,1,0:T(8,128)} %bitcast.61), kind=kOutput, calls=%fused_computation.37 | convolution fusion | flops 1610612736 | bytes 29360128 | tf_op jit(solution)/shard_map/cmn,cnk->cmk/dot_general | solution.py:59
  161.0 8.3 copy.74
  180.9 9.0 copy.79
  190.1 171.1 %all-to-all-done.1 = f32[32,2,256,128]{2,3,1,0:T(8,128)} async-done(((f32[32,2,256,128]{2,3,1,0:T(8,128)}), f32[32,2,256,128]{2,3,1,0:T(8,128)}, u32[]{:S(2)}, u32[]{:S(2)}) %all-to-all-start.1) | async-done | bytes 8388640 | tf_op jit(solution)/shard_map/all_to_all | solution.py:159
  361.2 8.9 copy.75
  370.1 20.8 %fusion.8 = f32[256,64,128]{2,0,1:T(8,128)S(1)} fusion(f32[256,256,1]{1,0,2:T(8,128)S(1)} %copy-done.5, f32[256,64,128]{2,1,0:T(8,128)} %bitcast.67), kind=kOutput, calls=%fused_computation.8 | convolution fusion | flops 3221225472 | bytes 17039360 | tf_op jit(solution)/shard_map/rh,hbk->rbk/dot_general | solution.py:55
  399.0 15.7 %broadcast_multiply_fusion.1 = (f32[128,128,128]{1,2,0:T(8,128)}, f32[128,128,128]{1,2,0:T(8,128)}) fusion(f32[128]{0:T(128)S(1)} %get-tuple-element.15, f32[128,128,128]{1,2,0:T(8,128)} %copy.79, f32[128,128]{1,0:T(8,128)S(1)} %copy.80, f32[128,128,128]{2,1,0:T(8,128)} %constant.80.clone, f32[128,128,128]{2,1,0:T(8,128)} %bitcast.70), kind=kOutput, calls=%fused_computation.23 | convolution fusion | flops 1616904192 | bytes 42009088 | tf_op jit(solution)/shard_map/cmn,cnk->cmk/dot_general | solution.py:59
  414.7 18.8 %fusion.2 = f32[128,128,256]{2,1,0:T(8,128)} fusion(f32[128,128,128]{2,1,0:T(8,128)} %constant.82.clone, f32[128,128,128]{1,2,0:T(8,128)} %get-tuple-element.14, f32[128,128,128]{1,2,0:T(8,128)} %get-tuple-element.13), kind=kOutput, calls=%fused_computation.2 | convolution fusion | flops 3225419776 | bytes 41943040 | tf_op jit(solution)/shard_map/cmn,cnk->cmk/dot_general | solution.py:59
  433.4 37.5 %fusion.6 = f32[256,64,256]{2,0,1:T(8,128)} fusion(f32[256,256,1]{1,0,2:T(8,128)S(1)} %copy-done.4, f32[256,64,256]{2,1,0:T(8,128)} %bitcast.63), kind=kOutput, calls=%fused_computation.6 | convolution fusion | flops 6442450944 | bytes 33816576 | tf_op jit(solution)/shard_map/rh,hbk->rbk/dot_general | solution.py:55
  471.0 17.7 %copy.83 = f32[256,64,256]{2,1,0:T(8,128)} copy(f32[256,64,256]{2,0,1:T(8,128)} %fusion.6) | data formatting | bytes 33554432 | tf_op jit(solution)/shard_map/rh,hbk->rbk/dot_general | solution.py:55
  504.8 360.6 %all-to-all-done.2 = f32[32,2,256,256]{3,2,1,0:T(8,128)} async-done(((f32[32,2,256,256]{3,2,1,0:T(8,128)}), f32[32,2,256,256]{3,2,1,0:T(8,128)}, u32[]{:S(2)}, u32[]{:S(2)}) %all-to-all-start.2) | async-done | bytes 16777248 | tf_op jit(solution)/shard_map/all_to_all | solution.py:192
  865.3 17.4 %copy.84 = f32[32,2,256,256]{2,3,1,0:T(8,128)} copy(f32[32,2,256,256]{3,2,1,0:T(8,128)} %all-to-all-done.2) | data formatting | bytes 33554432 | tf_op jit(solution)/shard_map/all_to_all | solution.py:192
  882.7 28.5 %copy.85 = f32[32,4,2,32,2,256]{5,4,3,2,1,0:T(2,128)} copy(f32[32,4,2,32,2,256]{5,3,1,4,2,0:T(8,128)} %bitcast.64) | data formatting | bytes 33554432 | tf_op jit(solution)/shard_map/transpose | solution.py:194
  911.2 21.6 %reshape.133 = f32[128,64,512]{2,1,0:T(8,128)} reshape(f32[32,4,2,32,2,256]{5,4,3,2,1,0:T(2,128)} %copy.85) | data formatting | bytes 33554432 | tf_op jit(solution)/shard_map/reshape | solution.py:198
  932.8 24.6 %fusion.23 = f32[128,128,512]{2,1,0:T(8,128)} fusion(f32[128,128,64]{1,2,0:T(8,128)} %constant.84.clone, f32[128,64,512]{2,1,0:T(8,128)} %reshape.133), kind=kOutput, calls=%fused_computation.38 | convolution fusion | flops 3221225472 | bytes 54525952 | tf_op jit(solution)/shard_map/cmn,cnk->cmk/dot_general | solution.py:59
  957.4 39.3 %fusion = f32[128,64,512]{2,0,1:T(8,128)S(1)} fusion(f32[128,256,1]{1,0,2:T(8,128)S(1)} %copy-done.6, f32[256,64,512]{2,1,0:T(8,128)} %bitcast.60), kind=kOutput, calls=%fused_computation | convolution fusion | flops 6442450944 | bytes 50462720 | tf_op jit(solution)/shard_map/rh,hbk->rbk/dot_general | solution.py:55
  1003.9 8.2 copy.87
  1047.0 55.8 %shard_map.118 = f32[8192,256]{1,0:T(8,128)S(1)} custom-call(f32[27]{0:T(128)S(1)} %reshape.122.weights_ref, f32[8192,256]{1,0:T(8,128)} %bitcast.49, f32[8192,256]{1,0:T(8,128)} %bitcast.50, f32[8192,256]{1,0:T(8,128)} %bitcast.51, f32[8192,256]{1,0:T(8,128)} %bitcast.53, f32[8192,256]{1,0:T(8,128)} %bitcast.54, f32[8192,256]{1,0:T(8,128)} %bitcast.55, ...), custom_call_target="tpu_custom_call" | custom-call | tf_op jit(solution)/shard_map/pallas_call | solution.py:113
  1102.7 96.9 %all_to_all.21 = f32[4,2048,256]{2,1,0:T(8,128)} all-to-all(f32[4,2048,256]{2,1,0:T(8,128)S(1)} %bitcast.46), channel_id=1, replica_groups=mesh['gx'=8,'gy'=4] {'gy'}, dimensions={0} | all-to-all | bytes 16777216 | tf_op jit(solution)/shard_map/all_to_all | solution.py:213
  1199.6 8.7 copy.92
  (50 shorter events, 77.8 us)
Async XLA Ops:
  101.2 8.7 copy-start.7
  169.2 5.9 copy-start.8
  169.2 192.0 %all-to-all-start.1 = ((f32[32,2,256,128]{2,3,1,0:T(8,128)}), f32[32,2,256,128]{2,3,1,0:T(8,128)}, u32[]{:S(2)}, u32[]{:S(2)}) async-start(f32[32,2,256,128]{2,3,1,0:T(8,128)} %bitcast.66), calls=%async_computation.1 | async-start | bytes 16777216 | tf_op jit(solution)/shard_map/all_to_all | solution.py:159
  180.9 9.0 copy-start.9
  190.0 180.1 %copy-start.5 = (f32[256,256,1]{1,0,2:T(8,128)S(1)}, f32[256,256,1]{1,0,2:T(8,128)}, u32[]{:S(2)}) copy-start(f32[256,256,1]{1,0,2:T(8,128)} %constant.92) | copy-start | bytes 786436
  414.7 18.8 %copy-start.4 = (f32[256,256,1]{1,0,2:T(8,128)S(1)}, f32[256,256,1]{1,0,2:T(8,128)}, u32[]{:S(2)}) copy-start(f32[256,256,1]{1,0,2:T(8,128)} %constant.91) | copy-start | bytes 786436
  488.7 376.6 %all-to-all-start.2 = ((f32[32,2,256,256]{3,2,1,0:T(8,128)}), f32[32,2,256,256]{3,2,1,0:T(8,128)}, u32[]{:S(2)}, u32[]{:S(2)}) async-start(f32[32,2,256,256]{3,2,1,0:T(8,128)} %bitcast.62), calls=%async_computation.2 | async-start | bytes 33554432 | tf_op jit(solution)/shard_map/all_to_all | solution.py:192
  499.4 533.3 %collective-permute-start = (f32[8192]{0:T(1024)S(1)}, f32[8192]{0:T(1024)S(1)}, u32[]{:S(2)}, u32[]{:S(2)}) collective-permute-start(f32[8192]{0:T(1024)S(1)} %get-tuple-element.10), channel_id=1, source_target_pairs={{0,1},{1,2},{2,3},{3,4},{4,5},{5,6},{6,7},{7,8},{8,9},{9,10},{10,1... | collective-permute-start | bytes 98312 | tf_op jit(solution)/shard_map/ppermute | solution.py:130
  499.5 538.7 %collective-permute-start.1 = (f32[8192]{0:T(1024)S(1)}, f32[8192]{0:T(1024)S(1)}, u32[]{:S(2)}, u32[]{:S(2)}) collective-permute-start(f32[8192]{0:T(1024)S(1)} %get-tuple-element.9), channel_id=1, source_target_pairs={{1,0},{2,1},{3,2},{4,3},{5,4},{6,5},{7,6},{8,7},{9,8},{10,9},{11,1... | collective-permute-start | bytes 98312 | tf_op jit(solution)/shard_map/ppermute | solution.py:131
  932.8 24.6 %copy-start.6 = (f32[128,256,1]{1,0,2:T(8,128)S(1)}, f32[128,256,1]{1,0,2:T(8,128)}, u32[]{:S(2)}) copy-start(f32[128,256,1]{1,0,2:T(8,128)} %constant.90) | copy-start | bytes 393220
  1012.2 17.1 %copy-start.2 = (f32[128,64,256]{2,1,0:T(8,128)}, f32[128,64,256]{2,1,0:T(8,128)S(1)}, u32[]{:S(2)}) copy-start(f32[128,64,256]{2,1,0:T(8,128)S(1)} %copy.87) | copy-start | bytes 25165828
  1015.5 22.6 %collective-permute-start.2 = (f32[8192]{0:T(1024)S(1)}, f32[8192]{0:T(1024)S(1)}, u32[]{:S(2)}, u32[]{:S(2)}) collective-permute-start(f32[8192]{0:T(1024)S(1)} %get-tuple-element.8), channel_id=1, source_target_pairs={{0,1},{1,2},{2,3},{3,4},{4,5},{5,6},{6,7},{7,8},{8,9},{9,10},{10,1... | collective-permute-start | bytes 98312 | tf_op jit(solution)/shard_map/ppermute | solution.py:130
  1015.6 22.6 %collective-permute-start.3 = (f32[8192]{0:T(1024)S(1)}, f32[8192]{0:T(1024)S(1)}, u32[]{:S(2)}, u32[]{:S(2)}) collective-permute-start(f32[8192]{0:T(1024)S(1)} %get-tuple-element.7), channel_id=1, source_target_pairs={{1,0},{2,1},{3,2},{4,3},{5,4},{6,5},{7,6},{8,7},{9,8},{10,9},{11,1... | collective-permute-start | bytes 98312 | tf_op jit(solution)/shard_map/ppermute | solution.py:131
  1029.3 3.4 copy-start.3
  1029.3 8.7 copy-start.10
  1032.6 7.0 collective-permute-start.4
  1032.7 6.9 collective-permute-start.5
  1042.6 2.2 copy-start
  1044.8 2.2 copy-start.1

commit v2 on v1

--- a/solution.py
+++ b/solution.py
@@ -176,31 +176,28 @@
     positive = squared > 0.0
     inverse = jnp.where(positive, 1.0 / jnp.where(positive, squared, 1.0), 0.0)
     potential = wave * inverse[:, None]
-    spectral = jnp.concatenate(
-        [potential * number_second, potential * -number_first[:, None]], axis=-1
-    )
-
     even = np.full((lead, tail), 1.0 / length)
-    back = tail_product(
-        tail_inverse(length, lead, even), spectral.reshape(lead, 2 * tail, 2 * waves)
-    )
+    columns_table = tail_inverse(length, lead, even)
     head_back = head.reshape(lead, 2, 2, lead).transpose(3, 2, 0, 1)
     mixed_back = head_back.reshape(devices, folds, 2, lead, 2).transpose(0, 2, 1, 3, 4)
-    back = head_product(
-        mixed_back.reshape(2 * lead, 2 * lead), back.reshape(2 * lead, tail, 2 * waves)
-    )
-    lines = lax.all_to_all(back.reshape(devices, 2, width, 2 * waves), BOTH, 0, 0)
-
-    lines = lines.reshape(devices, 2, width, 2, bands, half).transpose(0, 4, 1, 5, 3, 2)
+    mixed_back = mixed_back.reshape(2 * lead, 2 * lead)
     uneven = np.full((lead, half), 2.0 / length)
     uneven[0, 0] = 1.0 / length
-    speeds = tail_product(
-        tail_inverse(length, lead, uneven), lines.reshape(lead, 2 * half, 2 * width)
-    )
+    lines_table = tail_inverse(length, lead, uneven)
     last = -head_back[:, 1].reshape(lead, 2 * lead)
-    speeds = head_product(last, speeds.reshape(2 * lead, tail, 2 * width))
-    first = speeds[..., :width].reshape(length, width)
-    second = speeds[..., width:].reshape(length, width)
+    sent = []
+    for factor in (number_second, -number_first[:, None]):
+        spectral = (potential * factor).reshape(lead, 2 * tail, waves)
+        back = tail_product(columns_table, spectral)
+        back = head_product(mixed_back, back.reshape(2 * lead, tail, waves))
+        sent.append(lax.all_to_all(back.reshape(devices, 2, width, waves), BOTH, 0, 0))
+    speeds = []
+    for lines in sent:
+        lines = lines.swapaxes(2, 3).reshape(devices, 2, bands, half, width).swapaxes(1, 2)
+        speed = tail_product(lines_table, lines.reshape(lead, 2 * half, width))
+        speed = head_product(last, speed.reshape(2 * lead, tail, width))
+        speeds.append(speed.reshape(length, width))
+    first, second = speeds
 
     halo = []
     for cells in (field, first, second):

time: 1220 us -> 1070 us (0.88)
  waiting for transfers between devices: 533 us -> 454 us
  local copies, waits for them, and re-layouts: 206 us -> 140 us
    all_to_all x1 -> x2, waiting for transfers between devices: 361 us -> 270 us  [per_device(): lax.all_to_all(back.reshape(devices, 2, width, waves), BOTH, 0, 0)]
    slice x3 -> x0, local copies, waits for them, and re-layouts: 23.7 us -> none  [the longest x2 15.4 us: per_device(): second = speeds[..., width:].reshape(length, width)]
    reshape x1 -> x0, local copies, waits for them, and re-layouts: 21.6 us -> none  [per_device(): lines.reshape(lead, 2 * half, 2 * width)]
    all_to_all x1 -> x0, local copies, waits for them, and re-layouts: 17.4 us -> none  [per_device(): lax.all_to_all(back.reshape(devices, 2, width, 2 * waves), BOTH, 0, 0)]
    mul x4 -> x2, local copies, waits for them, and re-layouts: 13.7 us -> 0.09 us  [per_device(): spectral = (potential * factor).reshape(lead, 2 * tail, waves)]
    dot_general x4 -> x6, matrix products: 112 us -> 99 us  [head_product(): return jnp.einsum('rh,hbk->rbk', table, cells, precision=NEAR)]
    dot_general x3 -> x6, local copies, waits for them, and re-layouts: 46 us -> 54.4 us  [head_product(): return jnp.einsum('rh,hbk->rbk', table, cells, precision=NEAR)]
    dot_general x4 -> x6, matrix products: 74.9 us -> 78.6 us  [tail_product(): return jnp.einsum('cmn,cnk->cmk', table, cells, precision=NEAR)]
  transfers between devices with their start and end apart: 8 -> 9, of which waited for: 3 -> 4; matrix products, arithmetic and copies ran while one was open for 15% -> 14% of each run, Pallas kernels for 0% -> 0%
where the time goes in v2:
time: 1070 us; the launch traced here: 1060 us
  waiting for transfers between devices  454 us (42%)
  blocking collectives  198 us (19%)
  matrix products  178 us (17%)
  local copies, waits for them, and re-layouts  140 us (13%)
  Pallas kernels  55.8 us (5%)
  starting transfers between devices  29.6 us (3%)
    all_to_all x2, waiting for transfers between devices, per_device(): lax.all_to_all(back.reshape(devices, 2, width, waves), BOTH, 0, 0)  270 us
    all_to_all x1, waiting for transfers between devices, per_device(): lax.all_to_all(section.reshape(devices, 2, width, waves), BOTH, 0, 0)  183 us
    all_to_all x1, blocking collectives, per_device(): field = lax.all_to_all(turned, 'gy', 0, 0).reshape(length, width)  101 us
    dot_general x6, matrix products, head_product(): return jnp.einsum('rh,hbk->rbk', table, cells, precision=NEAR)  99 us
    all_to_all x1, blocking collectives, per_device(): rate = lax.all_to_all(rate.reshape(parts, columns, width), 'gy', 0, 0)  96.9 us
    dot_general x6, matrix products, tail_product(): return jnp.einsum('cmn,cnk->cmk', table, cells, precision=NEAR)  78.6 us
    pallas_call x1, Pallas kernels, stencil(): pl.pallas_call(body, grid=(length // rows,), in_specs=[pl.BlockSpec(memor...  55.8 us
    dot_general x6, local copies, waits for them, and re-layouts, head_product(): return jnp.einsum('rh,hbk->rbk', table, cells, precision=NEAR)  54.4 us
  transfers between devices with their start and end apart: 9, of which 4 were waited for; matrix products, arithmetic and copies ran while one was open for 14% of the time, Pallas kernels for 0%

profile of v2, /device:TPU:0, one launch (start us, length us, event | category | flops | bytes accessed | tf_op | source)
XLA Modules:
  0.0 1058.7 jit_solution(5125592393954575502)
XLA Ops:
  0.0 101.2 %all_to_all.25 = f32[4,2048,256]{1,2,0:T(8,128)} all-to-all(f32[4,2048,256]{1,2,0:T(8,128)} %bitcast.92), channel_id=1, replica_groups=mesh['gx'=8,'gy'=4] {'gy'}, dimensions={0} | all-to-all | bytes 16777216 | tf_op jit(solution)/shard_map/all_to_all | solution.py:149
  101.2 8.7 copy.79
  109.9 14.9 %fusion.10 = f32[256,64,256]{2,0,1:T(8,128)S(1)} fusion(f32[256,128,1]{1,0,2:T(8,128)S(1)} %copy-done.7, f32[128,64,256]{2,1,0:T(8,128)} %bitcast.63), kind=kOutput, calls=%fused_computation.11 | convolution fusion | flops 3221225472 | bytes 25296896 | tf_op jit(solution)/shard_map/rh,hbk->rbk/dot_general | solution.py:55
  124.8 20.3 %copy.82 = f32[256,64,256]{2,1,0:T(8,128)} copy(f32[256,64,256]{2,0,1:T(8,128)S(1)} %fusion.10) | data formatting | bytes 33554432 | tf_op jit(solution)/shard_map/rh,hbk->rbk/dot_general | solution.py:55
  145.1 15.9 %fusion.26 = f32[128,64,256]{2,1,0:T(8,128)} fusion(f32[128,64,128]{2,1,0:T(8,128)} %constant.78.clone, f32[128,128,256]{2,1,0:T(8,128)} %bitcast.78), kind=kOutput, calls=%fused_computation.40 | convolution fusion | flops 1610612736 | bytes 29360128 | tf_op jit(solution)/shard_map/cmn,cnk->cmk/dot_general | solution.py:59
  178.4 182.8 %all-to-all-done.1 = f32[32,2,256,128]{2,3,1,0:T(8,128)} async-done(((f32[32,2,256,128]{2,3,1,0:T(8,128)}), f32[32,2,256,128]{2,3,1,0:T(8,128)}, u32[]{:S(2)}, u32[]{:S(2)}) %all-to-all-start.1) | async-done | bytes 8388640 | tf_op jit(solution)/shard_map/all_to_all | solution.py:159
  361.2 8.9 copy.84
  370.1 20.8 %fusion.8 = f32[256,64,128]{2,0,1:T(8,128)S(1)} fusion(f32[256,256,1]{1,0,2:T(8,128)S(1)} %copy-done.6, f32[256,64,128]{2,1,0:T(8,128)} %bitcast.87), kind=kOutput, calls=%fused_computation.9 | convolution fusion | flops 3221225472 | bytes 17039360 | tf_op jit(solution)/shard_map/rh,hbk->rbk/dot_general | solution.py:55
  399.1 14.6 %bitcast_multiply_fusion = f32[128,128,128]{2,1,0:T(8,128)} fusion(f32[128,64,128]{2,1,0:T(8,128)} %fusion.16, f32[128,128,128]{2,1,0:T(8,128)} %constant.80.clone, f32[128,128,128]{2,1,0:T(8,128)} %bitcast.80), kind=kOutput, calls=%fused_computation.4 | convolution fusion | flops 1612709888 | bytes 29360128 | tf_op jit(solution)/shard_map/cmn,cnk->cmk/dot_general | solution.py:59
  413.6 13.7 %fusion.14 = f32[128,128,128]{2,1,0:T(8,128)} fusion(f32[128,128,128]{2,1,0:T(8,128)} %constant.82.clone, f32[128,128,128]{2,1,0:T(8,128)} %bitcast_multiply_fusion, f32[128]{0:T(128)S(1)} %get-tuple-element.11), kind=kOutput, calls=%fused_computation.15 | convolution fusion | flops 1612709888 | bytes 25166336 | tf_op jit(solution)/shard_map/cmn,cnk->cmk/dot_general | solution.py:59
  427.3 12.1 %fusion.6 = f32[256,64,128]{2,0,1:T(8,128)S(1)} fusion(f32[256,256,1]{1,0,2:T(8,128)S(1)} %copy-done.4, f32[256,64,128]{2,1,0:T(8,128)} %bitcast.88), kind=kOutput, calls=%fused_computation.7 | convolution fusion | flops 3221225472 | bytes 17039360 | tf_op jit(solution)/shard_map/rh,hbk->rbk/dot_general | solution.py:55
  451.5 9.5 fusion.12
  461.1 8.5 fusion.4
  477.9 159.7 %all-to-all-done.2 = f32[32,2,256,128]{3,2,1,0:T(8,128)} async-done(((f32[32,2,256,128]{3,2,1,0:T(8,128)}), f32[32,2,256,128]{3,2,1,0:T(8,128)}, u32[]{:S(2)}, u32[]{:S(2)}) %all-to-all-start.2) | async-done | bytes 8388640 | tf_op jit(solution)/shard_map/all_to_all | solution.py:193
  653.5 9.0 copy.89
  666.7 12.5 %fusion.27 = f32[128,128,256]{2,1,0:T(8,128)} fusion(f32[128,128,64]{1,2,0:T(8,128)} %constant.84.clone, f32[128,64,256]{2,1,0:T(8,128)S(1)} %bitcast.83), kind=kOutput, calls=%fused_computation.41 | convolution fusion | flops 1610612736 | bytes 29360128 | tf_op jit(solution)/shard_map/cmn,cnk->cmk/dot_general | solution.py:59
  679.2 21.4 %fusion.2 = f32[128,64,256]{2,0,1:T(8,128)S(1)} fusion(f32[128,256,1]{1,0,2:T(8,128)S(1)} %copy-done.5, f32[256,64,256]{2,1,0:T(8,128)} %bitcast.77), kind=kOutput, calls=%fused_computation.2 | convolution fusion | flops 3221225472 | bytes 25296896 | tf_op jit(solution)/shard_map/rh,hbk->rbk/dot_general | solution.py:55
  717.4 110.0 %all-to-all-done.3 = f32[32,2,256,128]{3,2,1,0:T(8,128)} async-done(((f32[32,2,256,128]{3,2,1,0:T(8,128)}), f32[32,2,256,128]{3,2,1,0:T(8,128)}, u32[]{:S(2)}, u32[]{:S(2)}) %all-to-all-start.3) | async-done | bytes 8388640 | tf_op jit(solution)/shard_map/all_to_all | solution.py:193
  827.4 9.0 copy.96
  840.6 12.5 %fusion.28 = f32[128,128,256]{2,1,0:T(8,128)} fusion(f32[128,128,64]{1,2,0:T(8,128)} %constant.84.clone, f32[128,64,256]{2,1,0:T(8,128)S(1)} %bitcast.82), kind=kOutput, calls=%fused_computation.42 | convolution fusion | flops 1610612736 | bytes 29360128 | tf_op jit(solution)/shard_map/cmn,cnk->cmk/dot_general | solution.py:59
  853.1 21.3 %fusion = f32[128,64,256]{2,0,1:T(8,128)S(1)} fusion(f32[128,256,1]{1,0,2:T(8,128)S(1)} %copy-done.5, f32[256,64,256]{2,1,0:T(8,128)} %bitcast.76), kind=kOutput, calls=%fused_computation | convolution fusion | flops 3221225472 | bytes 25296896 | tf_op jit(solution)/shard_map/rh,hbk->rbk/dot_general | solution.py:55
  896.9 55.8 %shard_map.154 = f32[8192,256]{1,0:T(8,128)S(1)} custom-call(f32[27]{0:T(128)S(1)} %reshape.136.weights_ref, f32[8192,256]{1,0:T(8,128)} %bitcast.65, f32[8192,256]{1,0:T(8,128)} %bitcast.66, f32[8192,256]{1,0:T(8,128)} %bitcast.67, f32[8192,256]{1,0:T(8,128)} %bitcast.69, f32[8192,256]{1,0:T(8,128)} %bitcast.70, f32[8192,256]{1,0:T(8,128)} %bitcast.71, ...), custom_call_target="tpu_custom_call" | custom-call | tf_op jit(solution)/shard_map/pallas_call | solution.py:113
  952.7 96.9 %all_to_all.26 = f32[4,2048,256]{2,1,0:T(8,128)} all-to-all(f32[4,2048,256]{2,1,0:T(8,128)S(1)} %bitcast.62), channel_id=1, replica_groups=mesh['gx'=8,'gy'=4] {'gy'}, dimensions={0} | all-to-all | bytes 16777216 | tf_op jit(solution)/shard_map/all_to_all | solution.py:210
  1049.6 8.7 copy.103
  (55 shorter events, 109.4 us)
Async XLA Ops:
  101.2 8.7 copy-start.7
  169.2 5.9 copy-start.8
  169.2 192.0 %all-to-all-start.1 = ((f32[32,2,256,128]{2,3,1,0:T(8,128)}), f32[32,2,256,128]{2,3,1,0:T(8,128)}, u32[]{:S(2)}, u32[]{:S(2)}) async-start(f32[32,2,256,128]{2,3,1,0:T(8,128)} %bitcast.85), calls=%async_computation.1 | async-start | bytes 16777216 | tf_op jit(solution)/shard_map/all_to_all | solution.py:159
  178.4 191.8 %copy-start.6 = (f32[256,256,1]{1,0,2:T(8,128)S(1)}, f32[256,256,1]{1,0,2:T(8,128)}, u32[]{:S(2)}) copy-start(f32[256,256,1]{1,0,2:T(8,128)} %constant.92) | copy-start | bytes 786436
  413.6 13.7 %copy-start.4 = (f32[256,256,1]{1,0,2:T(8,128)S(1)}, f32[256,256,1]{1,0,2:T(8,128)}, u32[]{:S(2)}) copy-start(f32[256,256,1]{1,0,2:T(8,128)} %constant.91) | copy-start | bytes 786436
  447.6 3.9 copy-start.9
  447.6 190.0 %all-to-all-start.2 = ((f32[32,2,256,128]{3,2,1,0:T(8,128)}), f32[32,2,256,128]{3,2,1,0:T(8,128)}, u32[]{:S(2)}, u32[]{:S(2)}) async-start(f32[32,2,256,128]{3,2,1,0:T(8,128)} %bitcast.86), calls=%async_computation.2 | async-start | bytes 16777216 | tf_op jit(solution)/shard_map/all_to_all | solution.py:193
  637.6 189.9 %all-to-all-start.3 = ((f32[32,2,256,128]{3,2,1,0:T(8,128)}), f32[32,2,256,128]{3,2,1,0:T(8,128)}, u32[]{:S(2)}, u32[]{:S(2)}) async-start(f32[32,2,256,128]{3,2,1,0:T(8,128)} %bitcast.84), calls=%async_computation.3 | async-start | bytes 16777216 | tf_op jit(solution)/shard_map/all_to_all | solution.py:193
  648.1 234.6 %collective-permute-start = (f32[8192]{0:T(1024)S(1)}, f32[8192]{0:T(1024)S(1)}, u32[]{:S(2)}, u32[]{:S(2)}) collective-permute-start(f32[8192]{0:T(1024)S(1)} %get-tuple-element.10), channel_id=1, source_target_pairs={{0,1},{1,2},{2,3},{3,4},{4,5},{5,6},{6,7},{7,8},{8,9},{9,10},{10,1... | collective-permute-start | bytes 98312 | tf_op jit(solution)/shard_map/ppermute | solution.py:130
  648.2 239.9 %collective-permute-start.1 = (f32[8192]{0:T(1024)S(1)}, f32[8192]{0:T(1024)S(1)}, u32[]{:S(2)}, u32[]{:S(2)}) collective-permute-start(f32[8192]{0:T(1024)S(1)} %get-tuple-element.9), channel_id=1, source_target_pairs={{1,0},{2,1},{3,2},{4,3},{5,4},{6,5},{7,6},{8,7},{9,8},{10,9},{11,1... | collective-permute-start | bytes 98312 | tf_op jit(solution)/shard_map/ppermute | solution.py:131
  666.7 12.5 %copy-start.5 = (f32[128,256,1]{1,0,2:T(8,128)S(1)}, f32[128,256,1]{1,0,2:T(8,128)}, u32[]{:S(2)}) copy-start(f32[128,256,1]{1,0,2:T(8,128)} %constant.90) | copy-start | bytes 393220
  705.4 3.2 copy-start.2
  712.0 176.1 %collective-permute-start.2 = (f32[8192]{0:T(1024)S(1)}, f32[8192]{0:T(1024)S(1)}, u32[]{:S(2)}, u32[]{:S(2)}) collective-permute-start(f32[8192]{0:T(1024)S(1)} %get-tuple-element.8), channel_id=1, source_target_pairs={{0,1},{1,2},{2,3},{3,4},{4,5},{5,6},{6,7},{7,8},{8,9},{9,10},{10,1... | collective-permute-start | bytes 98312 | tf_op jit(solution)/shard_map/ppermute | solution.py:130
  712.0 176.0 %collective-permute-start.3 = (f32[8192]{0:T(1024)S(1)}, f32[8192]{0:T(1024)S(1)}, u32[]{:S(2)}, u32[]{:S(2)}) collective-permute-start(f32[8192]{0:T(1024)S(1)} %get-tuple-element.7), channel_id=1, source_target_pairs={{1,0},{2,1},{3,2},{4,3},{5,4},{6,5},{7,6},{8,7},{9,8},{10,9},{11,1... | collective-permute-start | bytes 98312 | tf_op jit(solution)/shard_map/ppermute | solution.py:131
  879.2 3.4 copy-start.3
  879.2 8.7 copy-start.10
  882.6 7.0 collective-permute-start.4
  882.7 6.9 collective-permute-start.5
  892.5 2.2 copy-start
  894.7 2.2 copy-start.1
